TPU v7x, 512 devices: a whole 4x4x16 slice. The times are simulated.
512 devices in a mesh: dp: 128 (over y, z_lo, x, core), qsplit: 4 (over z_hi).
Axes of the slice: x: 4, y: 4, z: 16 (z_hi: 4, z_lo: 4; z = z_hi * 4 + z_lo), core: 2. Of those that a mesh axis runs over, the one named last changes fastest.
Arguments:
- scores: float32 [131072], P(('dp', 'qsplit')), may hold values from -6 to 6
- grades: int32 [131072], P(('dp', 'qsplit')), may hold values from 0 to 4
- lengths: int32 [128, 128], P('dp'), may hold values from 0 to 512, as said below
- bin_codes: int32 [700, 131072], P(None, ('dp', 'qsplit')), may hold values from 0 to 255
- node_ids: int32 [131072], P(('dp', 'qsplit')), may hold values from 0 to 1
Outputs:
- grad_rows: float32 [131072], P(('dp', 'qsplit'))
- hess_rows: float32 [131072], P(('dp', 'qsplit'))
- grad_hist: float32 [2, 179200], P(None, ('dp', 'qsplit'))
- hess_hist: float32 [2, 179200], P(None, ('dp', 'qsplit'))
Inputs may be any that keep to these rules, and one draw needn't show every extreme that they name: `lengths`: each row sums to 1024; every nonzero length is a multiple of 8; zeros only follow the last query of a row; every row holds one query of exactly 512 documents.
All inputs are finite; a program needn't handle non-finite values.
Results may differ from a plain program's by a relative error of at most 0.0003.
Values sent between devices are 32-bit elements; how exact they have to be, the bound alone decides.
A program may use at most 64 MiB of HBM per device.

v0:
```python
import math

import jax
import jax.numpy as jnp
from jax import lax
from jax.sharding import PartitionSpec as P

BINS = 256
NODES = 2
PAIR_TILE = 128


steepness = 1.0


def query_layout(length_row, group_rows):
    slot_ends = jnp.cumsum(length_row)
    slot_starts = slot_ends - length_row
    positions = jnp.arange(group_rows, dtype=jnp.int32)
    query_ids = jnp.searchsorted(slot_ends, positions, side="right")
    first_row = slot_starts[query_ids]
    last_end = slot_ends[query_ids]
    rank_pos = (positions - first_row).astype(jnp.float32)
    discount = 1.0 / jnp.log2(rank_pos + 2.0)
    return (query_ids, discount, first_row, last_end)


def pair_terms(own_score, own_gain, own_disc, own_query, far_score, far_gain, far_disc, far_query):
    spread = own_score[:, None] - far_score[None, :]
    gain_gap = own_gain[:, None] - far_gain[None, :]
    disc_gap = jnp.abs(own_disc[:, None] - far_disc[None, :])
    weight = jnp.where(own_query[:, None] == far_query[None, :], jnp.abs(gain_gap) * disc_gap, 0.0)
    direction = jnp.sign(gain_gap)
    pushed = weight * jax.nn.sigmoid(-direction * steepness * spread)
    curvature = weight * jax.nn.sigmoid(steepness * spread) * jax.nn.sigmoid(-steepness * spread)
    return (
        jnp.sum(-direction * pushed, axis=1),
        jnp.sum(pushed, axis=1),
        jnp.sum(curvature, axis=1),
    )


def shards(scores, grades, lengths, bin_codes, node_ids):
    row_count = scores.shape[0]
    split_count = lax.axis_size("qsplit")
    group_rows = row_count * split_count
    slot_count = lengths.shape[1]
    query_ids, discount, first_row, last_end = query_layout(lengths[0], group_rows)
    offset = lax.axis_index("qsplit") * row_count
    own_query = lax.dynamic_slice_in_dim(query_ids, offset, row_count)
    own_disc = lax.dynamic_slice_in_dim(discount, offset, row_count)
    gain_rows = jnp.exp2(grades.astype(jnp.float32)) - 1.0
    packed = jnp.stack([scores, gain_rows])
    tile_count = row_count // PAIR_TILE
    far_block = lax.all_gather(packed, "qsplit", axis=1, tiled=True)

    def own_tile(tile_index):
        tile_start = tile_index * PAIR_TILE
        own_score = lax.dynamic_slice_in_dim(scores, tile_start, PAIR_TILE)
        own_gain = lax.dynamic_slice_in_dim(gain_rows, tile_start, PAIR_TILE)
        tile_disc = lax.dynamic_slice_in_dim(own_disc, tile_start, PAIR_TILE)
        tile_query = lax.dynamic_slice_in_dim(own_query, tile_start, PAIR_TILE)
        return pair_terms(
            own_score,
            own_gain,
            tile_disc,
            tile_query,
            far_block[0],
            far_block[1],
            discount,
            query_ids,
        )

    slope_sum, push_sum, curv_sum = lax.map(own_tile, jnp.arange(tile_count, dtype=jnp.int32))
    slope_sum, push_sum, curv_sum = (slope_sum, push_sum, curv_sum)
    slope_sum = slope_sum.reshape(-1)
    push_sum = push_sum.reshape(-1)
    curv_sum = curv_sum.reshape(-1)
    choose = (own_query[:, None] == jnp.arange(slot_count, dtype=jnp.int32)[None, :]).astype(
        jnp.float32
    )
    partial_totals = jnp.dot(push_sum, choose, precision=lax.Precision.HIGHEST)
    totals = lax.psum(partial_totals, "qsplit")
    factor = jnp.log2(1.0 + totals) / jnp.maximum(totals, 1.0)
    row_factor = jnp.dot(choose, factor, precision=lax.Precision.HIGHEST)
    grad_rows = slope_sum * row_factor
    hess_rows = curv_sum * row_factor
    feature_count = bin_codes.shape[0]
    node_pick = (node_ids[None, :] == jnp.arange(NODES, dtype=jnp.int32)[:, None]).astype(
        jnp.float32
    )
    stat_rows = jnp.concatenate(
        [node_pick * grad_rows[None, :], node_pick * hess_rows[None, :]], axis=0
    )
    block_size = math.gcd(feature_count, 10)
    block_total = feature_count // block_size
    code_blocks = bin_codes.reshape(block_total, block_size, row_count)
    bin_range = jnp.arange(BINS, dtype=jnp.int32)

    def feature_block(codes):
        one_hot = (codes[:, :, None] == bin_range[None, None, :]).astype(jnp.float32)
        return jnp.einsum("kr,frb->kfb", stat_rows, one_hot, precision=lax.Precision.HIGHEST)

    per_block = lax.map(feature_block, code_blocks)
    hist_terms = jnp.transpose(per_block, (1, 0, 2, 3)).reshape(2, NODES, feature_count * BINS)
    summed = lax.psum_scatter(hist_terms, ("dp", "qsplit"), scatter_dimension=2, tiled=True)
    rows_per_bin = row_count * lax.axis_size("dp") * split_count // (NODES * BINS)
    summed = summed / math.sqrt(rows_per_bin)
    return (grad_rows, hess_rows, summed[0], summed[1])


def solution(mesh):
    return jax.shard_map(
        shards,
        mesh=mesh,
        in_specs=(
            P(("dp", "qsplit")),
            P(("dp", "qsplit")),
            P("dp", None),
            P(None, ("dp", "qsplit")),
            P(("dp", "qsplit")),
        ),
        out_specs=(
            P(("dp", "qsplit")),
            P(("dp", "qsplit")),
            P(None, ("dp", "qsplit")),
            P(None, ("dp", "qsplit")),
        ),
        check_vma=False,
    )
```

profile of v0, /device:TPU:2, one launch (start us, length us, event | category | flops | bytes accessed | tf_op | source)
XLA Modules:
  0.0 744.3 jit_solution(7342782072354190708)
XLA Ops:
  8.9 53.2 %while.51 = (s32[]{:T(128)}, u32[1024]{0:T(1024)S(1)}, u32[1024]{0:T(1024)S(1)}, s32[128]{0:T(128)S(1)}, s32[]{:T(128)}, /*index=5*/s32[]{:T(128)}, s32[]{}) while((s32[]{:T(128)}, u32[1024]{0:T(1024)S(1)}, u32[1024]{0:T(1024)S(1)}, s32[128]{0:T(128)S(1)}, s32[]{:T(128)}, /*index=5*/s32[]{:T(128)}, s32[]{}) %tuple.76), condition=%wide.region_2.3_spmd.clone, body=%wide.region_1.2_spmd.clone.sunk | while | flops 19460 | bytes 63589 | solution.py:20
  9.0 6.6 gather_fusion
  15.6 6.6 gather_fusion
  22.3 6.6 gather_fusion
  28.9 6.6 gather_fusion
  35.6 6.6 gather_fusion
  42.2 6.6 gather_fusion
  48.9 6.6 gather_fusion
  55.5 6.6 gather_fusion
  62.2 6.6 gather_fusion.1
  69.0 25.8 %all_gather.3 = f32[2,1024]{1,0:T(2,128)S(1)} all-gather(f32[2,256]{1,0:T(2,128)S(1)} %pad_maximum_fusion.1), channel_id=1, replica_groups=mesh['dp'=128,'qsplit'=4] {'qsplit'}, dimensions={1}, use_global_device_ids=true | all-gather | bytes 10240 | tf_op jit(solution)/shard_map/all_gather | solution.py:55
  94.8 5.1 while.49
  100.1 12.8 %psum.7 = f32[128]{0:T(128)S(1)} all-reduce(f32[128]{0:T(128)S(1)} %convolution_bitcast_fusion), channel_id=1, replica_groups=mesh['dp'=128,'qsplit'=4] {'qsplit'}, use_global_device_ids=true, to_apply=%region_8.9 | all-reduce | flops 128 | bytes 1024 | tf_op jit(solution)/shard_map/psum | solution.py:83
  113.1 2.3 reshape.70
  115.5 134.6 %while.50 = (s32[]{:T(128)}, f32[70,4,10,256]{3,1,2,0:T(4,128)S(1)}, s32[70,10,256]{2,1,0:T(8,128)}, f32[4,256]{1,0:T(4,128)S(1)}, s32[]{:T(128)}) while((s32[]{:T(128)}, f32[70,4,10,256]{3,1,2,0:T(4,128)S(1)}, s32[70,10,256]{2,1,0:T(8,128)}, f32[4,256]{1,0:T(4,128)S(1)}, s32[]{:T(128)}) %tuple.82), condition=%wide.region_10.11_spmd.clone, body=%wide.region_9.10_spmd.clone.sunk | while | flops 32112640 | bytes 81989 | solution.py:104
  116.2 1.2 fusion.53
  118.1 1.2 fusion.53
  120.1 1.2 fusion.53
  122.0 1.2 fusion.53
  123.9 1.2 fusion.53
  125.8 1.2 fusion.53
  127.7 1.2 fusion.53
  129.7 1.2 fusion.53
  131.6 1.2 fusion.53
  133.5 1.2 fusion.53
  135.4 1.2 fusion.53
  137.4 1.2 fusion.53
  139.3 1.2 fusion.53
  141.2 1.2 fusion.53
  143.1 1.2 fusion.53
  145.0 1.2 fusion.53
  147.0 1.2 fusion.53
  148.9 1.2 fusion.53
  150.8 1.2 fusion.53
  152.7 1.2 fusion.53
  154.7 1.2 fusion.53
  156.6 1.2 fusion.53
  158.5 1.2 fusion.53
  168.1 1.2 fusion.53
  181.6 1.2 fusion.53
  191.2 1.2 fusion.53
  204.7 1.2 fusion.53
  218.1 1.2 fusion.53
  227.7 1.2 fusion.53
  241.2 1.2 fusion.53
  250.1 2.8 copy.16
  252.8 4.8 reshape.71
  257.7 478.4 %all-reduce.3.cloned.1.call-done = f32[2,2,179200]{2,1,0:T(2,128)} async-done(((f32[2,2,179200]{2,1,0:T(2,128)}), f32[2,2,179200]{2,1,0:T(2,128)}) %all-reduce.3.cloned.1.call-update) | async-done | bytes 2867216
  (199 shorter events, 105.9 us)
Async XLA Ops:
  7.2 728.9 %all-reduce.3.cloned.1.call-start = ((), (), s32[]{:S(2)}) async-start(), calls=%async_computation | async-start | bytes 5734400
  62.1 6.8 copy-start.3
  62.2 6.8 copy-start.4
  94.8 20.6 %copy-start.2 = (s32[256]{0:T(256)S(1)}, s32[256]{0:T(256)}, u32[]{:S(2)}) copy-start(s32[256]{0:T(256)} %param.15) | copy-start | bytes 3076
  115.4 137.4 %copy-start = (f32[256]{0:T(256)}, f32[256]{0:T(256)S(1)}, u32[]{:S(2)}) copy-start(f32[256]{0:T(256)S(1)} %get-tuple-element.243) | copy-start | bytes 3076
  115.4 137.4 %copy-start.1 = (f32[256]{0:T(256)}, f32[256]{0:T(256)S(1)}, u32[]{:S(2)}) copy-start(f32[256]{0:T(256)S(1)} %get-tuple-element.244) | copy-start | bytes 3076
Sparse Core Ops, SparseCore 0:
  257.8 478.2 all-reduce.2
where the time goes:
time: 752 us; the launch traced here: 744 us
  waiting for transfers between devices  478 us (64%)
  local copies, waits for them, and re-layouts  123 us (16%)
  matrix products  83.4 us (11%)
  blocking collectives  38.6 us (5%)
  between operations  14.2 us (2%)
    unnamed x2, waiting for transfers between devices  478 us
    dot_general x70, matrix products, feature_block(): jnp.einsum('kr,frb->kfb', stat_rows, one_hot, precision=lax.Precision.HIG...  83 us
    gather x8, local copies, waits for them, and re-layouts, query_layout(): query_ids = jnp.searchsorted(slot_ends, positions, side='right')  52.6 us
    eq x70, local copies, waits for them, and re-layouts, feature_block(): codes[:, :, None] == bin_range[None, None, :]  50.6 us
    all_gather x1, blocking collectives, shards(): far_block = lax.all_gather(packed, 'qsplit', axis=1, tiled=True)  25.8 us
  transfers between devices with their start and end apart: 1, of which 1 were waited for; matrix products, arithmetic and copies ran while one was open for 0% of the time, Pallas kernels for 0%

commit v1 on v0

v1 whole, which is shorter than its diff:
```python
import jax
import jax.numpy as jnp
from jax import lax
from jax.experimental import pallas as pl
from jax.experimental.pallas import tpu as pltpu
from jax.sharding import PartitionSpec as P

F32, I32, BF16 = jnp.float32, jnp.int32, jnp.bfloat16
MESH = pl.DeviceIdType.MESH

FEATURES = 700
BINS = 256
PLANE = 32
DEPTH = 16
SPLIT = 4
TILES = 8
REACH = 4
SLOTS = 24
CHUNKS = 3
PER = SLOTS // CHUNKS
QUAD = 4
LOW = BINS // QUAD
WINDOW = 3
OWNED = FEATURES * BINS // (PLANE * DEPTH)
STEP = 8
LOG2E = 1.4426950408889634


def pieces(x):
    high = x.astype(BF16)
    rest = x - high.astype(F32)
    middle = rest.astype(BF16)
    return high, middle, (rest - middle.astype(F32)).astype(BF16)


def over_rows(x):
    return jnp.sum(x.reshape(x.shape[0] // 8, 8, x.shape[1]), axis=0)


def wait_bytes(ref, sem):
    pltpu.make_async_copy(ref, ref, sem).wait()


def kernel(
    score_ref, grade_ref, length_ref, codes_hbm, node_ref,
    grad_ref, hess_ref, grad_hist_ref, hess_hist_ref,
    codes_in, codes_tx, codes_rx, pack_tx, pack_rx, stat_tx, stat_rx, split,
    query, discount, score_all, gain_all, col_fixed, col_sent, same, hist, window_rx,
    load_sem, pack_send, pack_recv, code_send, code_recv, stat_send, stat_recv, final_send, final_recv,
):
    dp, part = lax.axis_index("dp"), lax.axis_index("qsplit")
    y, z_low, inner = dp // 32, (dp // 8) % 4, dp % 8
    me = y * 8 + inner
    level = z_low * 4 + part
    block, place = dp // 4, (dp % 4) * 4 + part

    def plane_peer(other):
        return ((other // 8) * 32 + z_low * 8 + other % 8, part)

    load = pltpu.make_async_copy(codes_hbm, codes_in, load_sem)
    load.start()

    barrier = pltpu.get_barrier_semaphore()

    def greet_plane(r, carry):
        pl.semaphore_signal(barrier, inc=1, device_id=plane_peer((me + r) % PLANE), device_id_type=MESH)
        return carry

    def greet_depth(r, carry):
        @pl.when(jnp.logical_or(r != level, me != block))
        def _():
            pl.semaphore_signal(
                barrier, inc=1, device_id=(y * 32 + (r // 4) * 8 + block % 8, r % 4), device_id_type=MESH
            )
        return carry

    for r in range(1, SPLIT):
        pl.semaphore_signal(barrier, inc=1, device_id=(dp, (part + r) % SPLIT), device_id_type=MESH)
    lax.fori_loop(0, DEPTH, greet_depth, 0)
    lax.fori_loop(1, PLANE, greet_plane, 0)

    gain = ((1 << grade_ref[...]) - 1).astype(F32)
    scaled = score_ref[...] * LOG2E
    pack_tx[0] = scaled
    pack_tx[1] = gain
    pack_rx[part] = pack_tx[...]

    pl.semaphore_wait(barrier, PLANE - 1 + SPLIT - 1 + DEPTH - jnp.where(me == block, 1, 0))

    packs = []
    for r in range(1, SPLIT):
        copy = pltpu.make_async_remote_copy(
            src_ref=pack_tx, dst_ref=pack_rx.at[part], send_sem=pack_send.at[r], recv_sem=pack_recv.at[part],
            device_id=(dp, (part + r) % SPLIT), device_id_type=MESH,
        )
        copy.start()
        packs.append(copy)

    load.wait()

    def lay(i, carry):
        at = pl.multiple_of(i * 8, 8)
        for h in range(2):
            codes_tx[pl.ds(at, 8), h, :] = codes_in[pl.ds(at, 8), 128 * h:128 * h + 128]
        return carry

    whole = FEATURES // 8
    lax.fori_loop(0, whole, lay, 0, unroll=4)
    for h in range(2):
        codes_tx[8 * whole:FEATURES, h, :] = codes_in[8 * whole:FEATURES, 128 * h:128 * h + 128]
    codes_tx[FEATURES:FEATURES + 4] = jnp.zeros((4, 2, 128), I32)

    def first_feature(other):
        return (other * 175) // 8

    for c in range(CHUNKS):
        def send_codes(r, carry, c=c):
            other = (me + r) % PLANE
            pltpu.make_async_remote_copy(
                src_ref=codes_tx.at[pl.ds(first_feature(other) + PER * c, PER)], dst_ref=codes_rx.at[c, me],
                send_sem=code_send.at[c], recv_sem=code_recv.at[c],
                device_id=plane_peer(other), device_id_type=MESH,
            ).start()
            return carry

        lax.fori_loop(1, PLANE, send_codes, 0)
        codes_rx[c, me] = codes_tx[pl.ds(first_feature(me) + PER * c, PER)]

    sub = lax.broadcasted_iota(I32, (128, 128), 0)
    lane = lax.broadcasted_iota(I32, (128, 128), 1)
    lengths = jnp.broadcast_to(length_ref[...].astype(F32) * 0.125, (128, 128))
    ends = 8.0 * jnp.dot(
        jnp.where(lane <= sub, lengths, 0.0).astype(BF16), jnp.ones((128, 128), BF16), preferred_element_type=F32
    )
    lane_row = lax.broadcasted_iota(I32, (1, 128), 1).astype(F32)
    for b in range(TILES):
        rows = lane_row + 128.0 * b
        done = ends <= rows
        query[b:b + 1, :] = jnp.sum(jnp.where(done, 1.0, 0.0), axis=0, keepdims=True)
        first = jnp.max(jnp.where(done, ends, 0.0), axis=0, keepdims=True)
        discount[b:b + 1, :] = 1.0 / jnp.log2(rows - first + 2.0)

    pick_row = lax.broadcasted_iota(I32, (32, 256), 0)
    pick_lane = lax.broadcasted_iota(I32, (32, 256), 1)
    side = (pick_row < 24) == (pick_lane < 128)

    def spread(first, second, out):
        stack = jnp.concatenate([*pieces(first), second.astype(BF16)], axis=0)
        for b in range(TILES):
            pick = jnp.where(jnp.logical_and(side, pick_row % 8 == b), 1.0, 0.0).astype(BF16)
            out[128 * b:128 * b + 128, :] = lax.dot_general(
                stack, pick, (((0,), (0,)), ((), ())), preferred_element_type=F32
            )

    spread(discount[...], query[...], col_fixed)
    own_query = [query[pl.ds(2 * part + h, 1), :] for h in range(2)]
    own_discount = [discount[pl.ds(2 * part + h, 1), :] for h in range(2)]
    for b in range(TILES):
        for h in range(2):
            same[128 * b:128 * b + 128, 128 * h:128 * h + 128] = jnp.where(
                col_fixed[128 * b:128 * b + 128, 128:256] == own_query[h], 1.0, 0.0
            ).astype(BF16)

    for r in range(1, SPLIT):
        source = (part + r) % SPLIT
        pltpu.make_async_remote_copy(
            src_ref=pack_tx, dst_ref=pack_rx.at[source], send_sem=pack_send.at[r], recv_sem=pack_recv.at[source],
            device_id=(dp, source), device_id_type=MESH,
        ).wait_recv()
    score_all[...] = jnp.concatenate([pack_rx[s, 0] for s in range(SPLIT)], axis=0)
    gain_all[...] = jnp.concatenate([pack_rx[s, 1] for s in range(SPLIT)], axis=0)
    spread(score_all[...], gain_all[...], col_sent)

    def pair(a, own_score, own_gain, own_disc, own_q):
        at = slice(128 * a, 128 * a + 128)
        gap = own_gain - col_sent[at, 128:256]
        diff = own_score - col_sent[at, 0:128]
        power = jnp.exp2(jnp.where(gap < 0.0, -diff, diff))
        ratio = 1.0 / (1.0 + power)
        weight = jnp.where(own_q == col_fixed[at, 128:256], jnp.abs(own_disc - col_fixed[at, 0:128]), 0.0)
        return gap * (weight * ratio), power * ratio

    totals = []
    for b in range(TILES):
        row = slice(b, b + 1)
        total = None
        for a in range(max(0, b - REACH), b + 1):
            slope, _ = pair(a, score_all[row, :], gain_all[row, :], discount[row, :], query[row, :])
            push = over_rows(jnp.abs(slope)) * (1.0 if a == b else 2.0)
            total = push if total is None else total + push
        totals.append(jnp.sum(total, axis=0, keepdims=True))
    stack = jnp.concatenate([*pieces(jnp.concatenate(totals, axis=0)), jnp.zeros((8, 128), BF16)], axis=0)
    stack_row = lax.broadcasted_iota(I32, (32, 128), 0)
    query_total = jnp.zeros((32, 256), F32)
    for b in range(TILES):
        query_total += jnp.dot(
            jnp.where(stack_row % 8 == b, stack, jnp.zeros_like(stack)), same[128 * b:128 * b + 128, :],
            preferred_element_type=F32,
        )
    query_total = jnp.sum(query_total, axis=0, keepdims=True)
    factor = jnp.log2(1.0 + query_total) / jnp.maximum(query_total, 1.0)

    stats = []
    for h in range(2):
        slope_sum, curv_sum = jnp.zeros((8, 128), F32), jnp.zeros((8, 128), F32)
        own_score, own_gain = score_all[pl.ds(2 * part + h, 1), :], gain_all[pl.ds(2 * part + h, 1), :]
        for a in range(TILES):
            slope, other = pair(a, own_score, own_gain, own_discount[h], own_query[h])
            slope_sum += over_rows(slope)
            curv_sum += over_rows(jnp.abs(slope) * other)
        own_factor = factor[:, 128 * h:128 * h + 128]
        grad = -jnp.sum(slope_sum, axis=0, keepdims=True) * own_factor
        hess = jnp.sum(curv_sum, axis=0, keepdims=True) * own_factor
        grad_ref[h:h + 1, :] = grad
        hess_ref[h:h + 1, :] = hess
        node = node_ref[h:h + 1, :]
        for value in (grad, hess):
            for n in range(2):
                stats.append(jnp.where(node == n, value, 0.0))
    stat_tx[...] = jnp.concatenate(stats, axis=0)

    def send_stats(r, carry):
        pltpu.make_async_remote_copy(
            src_ref=stat_tx, dst_ref=stat_rx.at[me], send_sem=stat_send, recv_sem=stat_recv,
            device_id=plane_peer((me + r) % PLANE), device_id_type=MESH,
        ).start()
        return carry

    lax.fori_loop(1, PLANE, send_stats, 0)
    stat_rx[me] = stat_tx[...]
    wait_bytes(stat_rx.at[pl.ds(0, PLANE - 1)], stat_recv)

    def prepare(s, carry):
        value = stat_rx[s]
        high = value.astype(BF16).astype(F32)
        low = value - high
        for h in range(2):
            a, b = high[4 * h:4 * h + 4], low[4 * h:4 * h + 4]
            split[s, :, 128 * h:128 * h + 128] = jnp.concatenate([a, b, a, b], axis=0).astype(BF16)
        return carry

    lax.fori_loop(0, PLANE, prepare, 0, unroll=4)

    row16 = lax.broadcasted_iota(I32, (16, 128), 0)
    highs = [(row16 // 8 + 2 * i).astype(BF16) for i in range(QUAD // 2)]
    lows = [(row16 + 16 * i).astype(BF16) for i in range(LOW // 16)]
    one, zero = jnp.ones((16, 128), BF16), jnp.zeros((16, 128), BF16)
    start = (me * 175 * 32) % BINS

    def operands(c, base, s):
        left, right = [], []
        for f in range(QUAD):
            left_half, right_half = [], []
            for h in range(2):
                code = codes_rx[c, s, base + f, h:h + 1, :]
                low = jnp.broadcast_to(code & (LOW - 1), (16, 128)).astype(BF16)
                high = jnp.broadcast_to(code >> 6, (16, 128)).astype(BF16)
                stat = split[s, :, 128 * h:128 * h + 128]
                left_half.append(jnp.concatenate([jnp.where(high == x, stat, zero) for x in highs], axis=0))
                right_half.append(jnp.concatenate([jnp.where(low == x, one, zero) for x in lows], axis=0))
            left.append(jnp.concatenate(left_half, axis=1))
            right.append(jnp.concatenate(right_half, axis=1))
        return jnp.concatenate(left, axis=0), jnp.concatenate(right, axis=0)

    def quad(g, carry):
        c, base = g // 2, (g % 2) * QUAD

        @pl.when(g % 2 == 0)
        def _():
            wait_bytes(codes_rx.at[c, pl.ds(0, PLANE - 1)], code_recv.at[c])

        def step(i, total):
            both = [operands(c, base, i * STEP + u) for u in range(STEP)]
            return total + lax.dot_general(
                jnp.concatenate([a for a, _ in both], axis=1), jnp.concatenate([b for _, b in both], axis=1),
                (((1,), (1,)), ((), ())), preferred_element_type=F32,
            )

        table = lax.fori_loop(0, PLANE // STEP, step, jnp.zeros((QUAD * QUAD * 8, BINS), F32))
        for f in range(QUAD):
            for high in range(QUAD):
                r = 8 * (QUAD * f + high)
                both = table[r:r + 8, LOW * f:LOW * f + LOW]
                hist[g * QUAD + f, :, LOW * high:LOW * high + LOW] = both[0:4] + both[4:8]

        def send_window(k, carry):
            j = 3 * g - 2 + k

            @pl.when(j >= 0)
            def _():
                slot = (start + j * OWNED) // BINS
                mine = jnp.logical_and(me == block, j == place)

                @pl.when(mine)
                def _():
                    window_rx[level] = hist[pl.ds(slot, WINDOW)]

                @pl.when(jnp.logical_not(mine))
                def _():
                    pltpu.make_async_remote_copy(
                        src_ref=hist.at[pl.ds(slot, WINDOW)], dst_ref=window_rx.at[level],
                        send_sem=final_send.at[j], recv_sem=final_recv.at[level],
                        device_id=(me * 4 + j // 4, j % 4), device_id_type=MESH,
                    ).start()
            return carry

        lax.fori_loop(0, 3, send_window, 0)
        return carry

    lax.fori_loop(0, SLOTS // QUAD, quad, 0)

    def arrive(k, total):
        @pl.when(jnp.logical_or(me != block, k != level))
        def _():
            wait_bytes(window_rx.at[k], final_recv.at[k])
        return total + window_rx[k]

    total = lax.fori_loop(0, DEPTH, arrive, jnp.zeros((WINDOW, 4, BINS), F32))
    line = jnp.concatenate([total[i] for i in range(WINDOW)], axis=1)
    line = jnp.concatenate([line, line], axis=0) * (1.0 / 16.0)
    offset = ((block * 175 * 32) % BINS + place * OWNED) % BINS
    line = pltpu.roll(line, WINDOW * BINS - offset, 1)
    grad_hist_ref[...] = line[0:2, 0:OWNED]
    hess_hist_ref[...] = line[2:4, 0:OWNED]

    for copy in packs:
        copy.wait_send()
    for c in range(CHUNKS):
        wait_bytes(codes_rx.at[c, pl.ds(0, PLANE - 1)], code_send.at[c])
    wait_bytes(stat_rx.at[pl.ds(0, PLANE - 1)], stat_send)

    def sent(j, carry):
        @pl.when(jnp.logical_or(me != block, j != place))
        def _():
            wait_bytes(window_rx.at[j], final_send.at[j])
        return carry

    lax.fori_loop(0, DEPTH, sent, 0)


def shards(scores, grades, lengths, bin_codes, node_ids):
    vmem = pl.BlockSpec(memory_space=pltpu.VMEM)
    dma = pltpu.SemaphoreType.DMA
    rows = 2, 128
    grad, hess, grad_hist, hess_hist = pl.pallas_call(
        kernel,
        out_shape=[
            jax.ShapeDtypeStruct(rows, F32),
            jax.ShapeDtypeStruct(rows, F32),
            jax.ShapeDtypeStruct((2, OWNED), F32),
            jax.ShapeDtypeStruct((2, OWNED), F32),
        ],
        in_specs=[vmem, vmem, vmem, pl.BlockSpec(memory_space=pl.ANY), vmem],
        out_specs=[vmem] * 4,
        scratch_shapes=[
            pltpu.VMEM((FEATURES, 256), I32),
            pltpu.VMEM((FEATURES + 4, 2, 128), I32),
            pltpu.VMEM((CHUNKS, PLANE, PER, 2, 128), I32),
            pltpu.VMEM((2, 2, 128), F32),
            pltpu.VMEM((SPLIT, 2, 2, 128), F32),
            pltpu.VMEM((8, 128), F32),
            pltpu.VMEM((PLANE, 8, 128), F32),
            pltpu.VMEM((PLANE, 16, 256), BF16),
            pltpu.VMEM((8, 128), F32),
            pltpu.VMEM((8, 128), F32),
            pltpu.VMEM((8, 128), F32),
            pltpu.VMEM((8, 128), F32),
            pltpu.VMEM((128 * TILES, 256), F32),
            pltpu.VMEM((128 * TILES, 256), F32),
            pltpu.VMEM((128 * TILES, 256), BF16),
            pltpu.VMEM((SLOTS, 4, BINS), F32),
            pltpu.VMEM((DEPTH, WINDOW, 4, BINS), F32),
            dma,
            dma((SPLIT,)),
            dma((SPLIT,)),
            dma((CHUNKS,)),
            dma((CHUNKS,)),
            dma,
            dma,
            dma((DEPTH,)),
            dma((DEPTH,)),
        ],
        compiler_params=pltpu.CompilerParams(
            collective_id=0, has_side_effects=True, vmem_limit_bytes=40 * 2**20
        ),
        cost_estimate=pl.CostEstimate(flops=10**9, bytes_accessed=10**6, transcendentals=10**6),
    )(scores.reshape(rows), grades.reshape(rows), lengths, bin_codes, node_ids.reshape(rows))
    return grad.reshape(-1), hess.reshape(-1), grad_hist, hess_hist


def solution(mesh):
    rows = P(("dp", "qsplit"))
    bins = P(None, ("dp", "qsplit"))
    return jax.shard_map(
        shards,
        mesh=mesh,
        in_specs=(rows, rows, P("dp", None), bins, rows),
        out_specs=(rows, rows, bins, bins),
        check_vma=False,
    )
```

time: 752 us -> 58.8 us (0.08)
  waiting for transfers between devices: 478 us -> 0 us
  local copies, waits for them, and re-layouts: 123 us -> 4.07 us
  matrix products: 83.4 us -> 0 us
  Pallas kernels: 0 us -> 53 us
  blocking collectives: 38.6 us -> 0 us
  between operations: 14.2 us -> 0.68 us
    unnamed x2 -> x0, waiting for transfers between devices: 478 us -> none
    dot_general x72 -> x0, matrix products: 83.4 us -> none  [the longest x70 83 us: feature_block(): jnp.einsum('kr,frb->kfb', stat_rows, one_hot, precision=lax.Precision.HIG...]
    gather x9 -> x0, local copies, waits for them, and re-layouts: 59.1 us -> none  [the longest x8 52.6 us: query_layout(): query_ids = jnp.searchsorted(slot_ends, positions, side='right')]
    pallas_call x0 -> x1, Pallas kernels: none -> 53 us  [shards(): pl.pallas_call(kernel, out_shape=[jax.ShapeDtypeStruct(rows, F32), jax.Sh...]
    eq x70 -> x0, local copies, waits for them, and re-layouts: 50.6 us -> none  [feature_block(): codes[:, :, None] == bin_range[None, None, :]]
    all_gather x1 -> x0, blocking collectives: 25.8 us -> none  [shards(): far_block = lax.all_gather(packed, 'qsplit', axis=1, tiled=True)]
    psum x1 -> x0, blocking collectives: 12.8 us -> none  [shards(): totals = lax.psum(partial_totals, 'qsplit')]
  transfers between devices with their start and end apart: 1 -> 0, of which waited for: 1 -> 0; matrix products, arithmetic and copies ran while one was open for 0% -> 0% of each run, Pallas kernels for 0% -> 0%
where the time goes in v1:
time: 58.8 us; the launch traced here: 57.8 us
  Pallas kernels  53 us (90%)
  local copies, waits for them, and re-layouts  4.07 us (7%)
  between operations  0.68 us (1%)
    pallas_call x1, Pallas kernels, shards(): pl.pallas_call(kernel, out_shape=[jax.ShapeDtypeStruct(rows, F32), jax.Sh...  53 us
    unnamed x14, local copies, waits for them, and re-layouts  4.07 us

profile of v1, /device:TPU:2, one launch (start us, length us, event | category | flops | bytes accessed | tf_op | source)
XLA Modules:
  0.0 57.8 jit_solution(10384847641481429438)
XLA Ops:
  0.6 0.0 copy-start.2
  0.6 0.0 copy-start.3
  0.7 0.0 copy-start.1
  0.7 0.0 copy-start.4
  0.7 0.6 %copy-done.2 = s32[256]{0:T(256)S(1)} copy-done((s32[256]{0:T(256)S(1)}, s32[256]{0:T(256)}, u32[]{:S(2)}) %copy-start.2) | copy-done | bytes 1048
  1.3 0.0 copy-done.3
  1.3 0.0 copy-done.1
  1.3 0.0 copy-done.4
  1.3 0.0 copy-start
  1.3 1.1 %copy-done = s32[700,256]{1,0:T(8,128)S(1)} copy-done((s32[700,256]{1,0:T(8,128)S(1)}, s32[700,256]{1,0:T(8,128)}, u32[]{:S(2)}) %copy-start) | copy-done | bytes 716824
  2.5 53.0 %shard_map.84 = (f32[2,128]{1,0:T(2,128)S(1)}, f32[2,128]{1,0:T(2,128)S(1)}, f32[2,350]{1,0:T(2,128)S(1)}, f32[2,350]{1,0:T(2,128)S(1)}) custom-call(f32[2,128]{1,0:T(2,128)S(1)} %bitcast.7, s32[2,128]{1,0:T(2,128)S(1)} %bitcast.8, s32[1,128]{1,0:T(1,128)S(1)} %copy-done.4, s32[700,256]{1,0:T(8,128)S(1)} %copy-done, s32[2,128]{1,0:T(2,128)S(1)} %bitcast.9), custom_call_target="tpu_custom_call" | custom-call | flops 1000000000 | bytes 1000000 | tf_op jit(solution)/shard_map/pallas_call | solution.py:345
  55.5 0.6 copy.13
  56.0 0.6 copy.14
  56.6 0.6 copy.15
  57.2 0.6 copy.16
Async XLA Ops:
  0.6 0.7 %copy-start.2 = (s32[256]{0:T(256)S(1)}, s32[256]{0:T(256)}, u32[]{:S(2)}) copy-start(s32[256]{0:T(256)} %param.6) | copy-start | bytes 3076
  0.6 0.7 %copy-start.3 = (s32[256]{0:T(256)S(1)}, s32[256]{0:T(256)}, u32[]{:S(2)}) copy-start(s32[256]{0:T(256)} %param.9) | copy-start | bytes 3076
  0.7 0.7 %copy-start.1 = (f32[256]{0:T(256)S(1)}, f32[256]{0:T(256)}, u32[]{:S(2)}) copy-start(f32[256]{0:T(256)} %param.5) | copy-start | bytes 3076
  0.7 0.7 %copy-start.4 = (s32[1,128]{1,0:T(1,128)S(1)}, s32[1,128]{1,0:T(1,128)}, u32[]{:S(2)}) copy-start(s32[1,128]{1,0:T(1,128)} %length_ref.1) | copy-start | bytes 1540
  1.3 1.1 %copy-start = (s32[700,256]{1,0:T(8,128)S(1)}, s32[700,256]{1,0:T(8,128)}, u32[]{:S(2)}) copy-start(s32[700,256]{1,0:T(8,128)} %codes_hbm.1) | copy-start | bytes 2150404

commit v2 on v1

--- a/solution.py
+++ b/solution.py
@@ -16,13 +16,11 @@
 TILES = 8
 REACH = 4
 SLOTS = 24
-CHUNKS = 3
-PER = SLOTS // CHUNKS
 QUAD = 4
 LOW = BINS // QUAD
 WINDOW = 3
+WIDE = 384
 OWNED = FEATURES * BINS // (PLANE * DEPTH)
-STEP = 8
 LOG2E = 1.4426950408889634
 
 
@@ -37,47 +35,75 @@
     return jnp.sum(x.reshape(x.shape[0] // 8, 8, x.shape[1]), axis=0)
 
 
+def inverse(x):
+    guess = pl.reciprocal(x, approx=True)
+    return guess * (2.0 - x * guess)
+
+
 def wait_bytes(ref, sem):
     pltpu.make_async_copy(ref, ref, sem).wait()
 
 
+def feature_block(inner):
+    x, core = inner // 2, inner % 2
+    return 4 * (x % 2) + 2 * core + x // 2
+
+
+def summing_device(eighth):
+    x, core = 2 * (eighth % 2) + eighth // 4, (eighth // 2) % 2
+    return 2 * x + core
+
+
 def kernel(
-    score_ref, grade_ref, length_ref, codes_hbm, node_ref,
-    grad_ref, hess_ref, grad_hist_ref, hess_hist_ref,
-    codes_in, codes_tx, codes_rx, pack_tx, pack_rx, stat_tx, stat_rx, split,
-    query, discount, score_all, gain_all, col_fixed, col_sent, same, hist, window_rx,
+    score_hbm, grade_hbm, length_hbm, codes_hbm, node_hbm,
+    out_ref,
+    score_ref, grade_ref, length_ref, codes_in, node_ref,
+    codes_tx, codes_rx, pack_tx, pack_rx, stat_tx, stat_rx, split,
+    query, discount, score_all, gain_all, col_fixed, col_sent, same, hist, window_tx, window_rx,
     load_sem, pack_send, pack_recv, code_send, code_recv, stat_send, stat_recv, final_send, final_recv,
 ):
     dp, part = lax.axis_index("dp"), lax.axis_index("qsplit")
     y, z_low, inner = dp // 32, (dp // 8) % 4, dp % 8
     me = y * 8 + inner
     level = z_low * 4 + part
+    sums = y * 8 + feature_block(inner)
     block, place = dp // 4, (dp % 4) * 4 + part
 
     def plane_peer(other):
         return ((other // 8) * 32 + z_low * 8 + other % 8, part)
 
-    load = pltpu.make_async_copy(codes_hbm, codes_in, load_sem)
-    load.start()
+    def away(r):
+        return (me + 1 + (r + 9) % (PLANE - 1)) % PLANE
+
+    loads = []
+    for i, (source, target) in enumerate((
+        (score_hbm, score_ref), (grade_hbm, grade_ref), (length_hbm, length_ref), (node_hbm, node_ref),
+        (codes_hbm, codes_in),
+    )):
+        loads.append(pltpu.make_async_copy(source, target, load_sem.at[i]))
+        loads[-1].start()
 
     barrier = pltpu.get_barrier_semaphore()
 
     def greet_plane(r, carry):
-        pl.semaphore_signal(barrier, inc=1, device_id=plane_peer((me + r) % PLANE), device_id_type=MESH)
+        pl.semaphore_signal(barrier, inc=1, device_id=plane_peer(away(r)), device_id_type=MESH)
         return carry
 
     def greet_depth(r, carry):
-        @pl.when(jnp.logical_or(r != level, me != block))
+        @pl.when(jnp.logical_or(r != level, sums != block))
         def _():
             pl.semaphore_signal(
-                barrier, inc=1, device_id=(y * 32 + (r // 4) * 8 + block % 8, r % 4), device_id_type=MESH
+                barrier, inc=1, device_id=(y * 32 + (r // 4) * 8 + summing_device(block % 8), r % 4), device_id_type=MESH
             )
         return carry
 
     for r in range(1, SPLIT):
         pl.semaphore_signal(barrier, inc=1, device_id=(dp, (part + r) % SPLIT), device_id_type=MESH)
     lax.fori_loop(0, DEPTH, greet_depth, 0)
-    lax.fori_loop(1, PLANE, greet_plane, 0)
+    lax.fori_loop(0, PLANE - 1, greet_plane, 0)
+
+    for load in loads[:4]:
+        load.wait()
 
     gain = ((1 << grade_ref[...]) - 1).astype(F32)
     scaled = score_ref[...] * LOG2E
@@ -85,7 +111,7 @@
     pack_tx[1] = gain
     pack_rx[part] = pack_tx[...]
 
-    pl.semaphore_wait(barrier, PLANE - 1 + SPLIT - 1 + DEPTH - jnp.where(me == block, 1, 0))
+    pl.semaphore_wait(barrier, PLANE - 1 + SPLIT - 1 + DEPTH - jnp.where(sums == block, 1, 0))
 
     packs = []
     for r in range(1, SPLIT):
@@ -96,7 +122,7 @@
         copy.start()
         packs.append(copy)
 
-    load.wait()
+    loads[4].wait()
 
     def lay(i, carry):
         at = pl.multiple_of(i * 8, 8)
@@ -110,21 +136,21 @@
         codes_tx[8 * whole:FEATURES, h, :] = codes_in[8 * whole:FEATURES, 128 * h:128 * h + 128]
     codes_tx[FEATURES:FEATURES + 4] = jnp.zeros((4, 2, 128), I32)
 
-    def first_feature(other):
-        return (other * 175) // 8
-
-    for c in range(CHUNKS):
-        def send_codes(r, carry, c=c):
-            other = (me + r) % PLANE
-            pltpu.make_async_remote_copy(
-                src_ref=codes_tx.at[pl.ds(first_feature(other) + PER * c, PER)], dst_ref=codes_rx.at[c, me],
-                send_sem=code_send.at[c], recv_sem=code_recv.at[c],
-                device_id=plane_peer(other), device_id_type=MESH,
-            ).start()
-            return carry
-
-        lax.fori_loop(1, PLANE, send_codes, 0)
-        codes_rx[c, me] = codes_tx[pl.ds(first_feature(me) + PER * c, PER)]
+    def codes_for(other):
+        first = ((other // 8) * 8 + feature_block(other % 8)) * 175 // 8
+        return codes_tx.at[pl.ds(first, SLOTS)]
+
+    def send_codes(r, carry):
+        other = away(r)
+        pltpu.make_async_remote_copy(
+            src_ref=codes_for(other), dst_ref=codes_rx.at[me], send_sem=code_send, recv_sem=code_recv,
+            device_id=plane_peer(other), device_id_type=MESH,
+        ).start()
+        return carry
+
+    lax.fori_loop(0, PLANE - 1, send_codes, 0)
+    codes_rx[me] = codes_for(me)[...]
+    hist[...] = jnp.zeros_like(hist)
 
     sub = lax.broadcasted_iota(I32, (128, 128), 0)
     lane = lax.broadcasted_iota(I32, (128, 128), 1)
@@ -176,7 +202,7 @@
         gap = own_gain - col_sent[at, 128:256]
         diff = own_score - col_sent[at, 0:128]
         power = jnp.exp2(jnp.where(gap < 0.0, -diff, diff))
-        ratio = 1.0 / (1.0 + power)
+        ratio = inverse(1.0 + power)
         weight = jnp.where(own_q == col_fixed[at, 128:256], jnp.abs(own_disc - col_fixed[at, 0:128]), 0.0)
         return gap * (weight * ratio), power * ratio
 
@@ -211,8 +237,8 @@
         own_factor = factor[:, 128 * h:128 * h + 128]
         grad = -jnp.sum(slope_sum, axis=0, keepdims=True) * own_factor
         hess = jnp.sum(curv_sum, axis=0, keepdims=True) * own_factor
-        grad_ref[h:h + 1, :] = grad
-        hess_ref[h:h + 1, :] = hess
+        out_ref[4 + h:5 + h, 0:128] = grad
+        out_ref[6 + h:7 + h, 0:128] = hess
         node = node_ref[h:h + 1, :]
         for value in (grad, hess):
             for n in range(2):
@@ -222,11 +248,11 @@
     def send_stats(r, carry):
         pltpu.make_async_remote_copy(
             src_ref=stat_tx, dst_ref=stat_rx.at[me], send_sem=stat_send, recv_sem=stat_recv,
-            device_id=plane_peer((me + r) % PLANE), device_id_type=MESH,
+            device_id=plane_peer(away(r)), device_id_type=MESH,
         ).start()
         return carry
 
-    lax.fori_loop(1, PLANE, send_stats, 0)
+    lax.fori_loop(0, PLANE - 1, send_stats, 0)
     stat_rx[me] = stat_tx[...]
     wait_bytes(stat_rx.at[pl.ds(0, PLANE - 1)], stat_recv)
 
@@ -245,117 +271,128 @@
     highs = [(row16 // 8 + 2 * i).astype(BF16) for i in range(QUAD // 2)]
     lows = [(row16 + 16 * i).astype(BF16) for i in range(LOW // 16)]
     one, zero = jnp.ones((16, 128), BF16), jnp.zeros((16, 128), BF16)
-    start = (me * 175 * 32) % BINS
-
-    def operands(c, base, s):
+    start = (sums * 175 * 32) % BINS
+
+    def first_slot(j):
+        return (start + j * OWNED) // BINS
+
+    def slot_at(i):
+        early = first_slot(4 * (i // 3)) + i % 3
+        late = i - 9
+        for k in (4, 8, 12):
+            late = late + jnp.where(late >= first_slot(k), 3, 0)
+        return jnp.where(i < 12, early, late)
+
+    def quad_of(j):
+        early = jnp.where(j >= 8, 2, j // 4)
+        late = jnp.where(j < 4, 3, jnp.where(j < 12, 4, 5))
+        return jnp.where(j % 4 == 0, early, late)
+
+    def operands(slots, s):
         left, right = [], []
-        for f in range(QUAD):
+        for slot in slots:
             left_half, right_half = [], []
             for h in range(2):
-                code = codes_rx[c, s, base + f, h:h + 1, :]
+                code = codes_rx[s, slot, h:h + 1, :]
                 low = jnp.broadcast_to(code & (LOW - 1), (16, 128)).astype(BF16)
                 high = jnp.broadcast_to(code >> 6, (16, 128)).astype(BF16)
                 stat = split[s, :, 128 * h:128 * h + 128]
-                left_half.append(jnp.concatenate([jnp.where(high == x, stat, zero) for x in highs], axis=0))
-                right_half.append(jnp.concatenate([jnp.where(low == x, one, zero) for x in lows], axis=0))
+                left_half.append(jnp.concatenate([jnp.where(low == x, one, zero) for x in lows], axis=0))
+                right_half.append(jnp.concatenate([jnp.where(high == x, stat, zero) for x in highs], axis=0))
             left.append(jnp.concatenate(left_half, axis=1))
             right.append(jnp.concatenate(right_half, axis=1))
         return jnp.concatenate(left, axis=0), jnp.concatenate(right, axis=0)
 
+    wait_bytes(codes_rx.at[pl.ds(0, PLANE - 1)], code_recv)
+
     def quad(g, carry):
-        c, base = g // 2, (g % 2) * QUAD
-
-        @pl.when(g % 2 == 0)
-        def _():
-            wait_bytes(codes_rx.at[c, pl.ds(0, PLANE - 1)], code_recv.at[c])
-
-        def step(i, total):
-            both = [operands(c, base, i * STEP + u) for u in range(STEP)]
-            return total + lax.dot_general(
-                jnp.concatenate([a for a, _ in both], axis=1), jnp.concatenate([b for _, b in both], axis=1),
-                (((1,), (1,)), ((), ())), preferred_element_type=F32,
-            )
-
-        table = lax.fori_loop(0, PLANE // STEP, step, jnp.zeros((QUAD * QUAD * 8, BINS), F32))
+        slots = [slot_at(g * QUAD + f) for f in range(QUAD)]
+        both = [operands(slots, s) for s in range(PLANE)]
+        table = lax.dot_general(
+            jnp.concatenate([a for a, _ in both], axis=1), jnp.concatenate([b for _, b in both], axis=1),
+            (((1,), (1,)), ((), ())), preferred_element_type=F32,
+        ).T
         for f in range(QUAD):
             for high in range(QUAD):
                 r = 8 * (QUAD * f + high)
-                both = table[r:r + 8, LOW * f:LOW * f + LOW]
-                hist[g * QUAD + f, :, LOW * high:LOW * high + LOW] = both[0:4] + both[4:8]
-
-        def send_window(k, carry):
-            j = 3 * g - 2 + k
-
-            @pl.when(j >= 0)
+                halves = table[r:r + 8, LOW * f:LOW * f + LOW]
+                hist[slots[f], :, LOW * high:LOW * high + LOW] = halves[0:4] + halves[4:8]
+
+        def send_window(j, carry):
+            @pl.when(quad_of(j) == g)
             def _():
-                slot = (start + j * OWNED) // BINS
-                mine = jnp.logical_and(me == block, j == place)
+                at = first_slot(j)
+                line = jnp.concatenate([hist[at + i] for i in range(WINDOW)], axis=1)
+                line = jnp.concatenate([line, line], axis=0)
+                line = pltpu.roll(line, WINDOW * BINS - (start + j * OWNED) % BINS, 1)[0:4, 0:WIDE]
+                mine = jnp.logical_and(sums == block, j == place)
 
                 @pl.when(mine)
                 def _():
-                    window_rx[level] = hist[pl.ds(slot, WINDOW)]
+                    window_rx[level] = line
 
                 @pl.when(jnp.logical_not(mine))
                 def _():
+                    window_tx[j] = line
                     pltpu.make_async_remote_copy(
-                        src_ref=hist.at[pl.ds(slot, WINDOW)], dst_ref=window_rx.at[level],
+                        src_ref=window_tx.at[j], dst_ref=window_rx.at[level],
                         send_sem=final_send.at[j], recv_sem=final_recv.at[level],
-                        device_id=(me * 4 + j // 4, j % 4), device_id_type=MESH,
+                        device_id=(sums * 4 + j // 4, j % 4), device_id_type=MESH,
                     ).start()
             return carry
 
-        lax.fori_loop(0, 3, send_window, 0)
+        lax.fori_loop(0, DEPTH, send_window, 0)
         return carry
 
     lax.fori_loop(0, SLOTS // QUAD, quad, 0)
 
     def arrive(k, total):
-        @pl.when(jnp.logical_or(me != block, k != level))
+        @pl.when(jnp.logical_or(sums != block, k != level))
         def _():
             wait_bytes(window_rx.at[k], final_recv.at[k])
         return total + window_rx[k]
 
-    total = lax.fori_loop(0, DEPTH, arrive, jnp.zeros((WINDOW, 4, BINS), F32))
-    line = jnp.concatenate([total[i] for i in range(WINDOW)], axis=1)
-    line = jnp.concatenate([line, line], axis=0) * (1.0 / 16.0)
-    offset = ((block * 175 * 32) % BINS + place * OWNED) % BINS
-    line = pltpu.roll(line, WINDOW * BINS - offset, 1)
-    grad_hist_ref[...] = line[0:2, 0:OWNED]
-    hess_hist_ref[...] = line[2:4, 0:OWNED]
+    total = lax.fori_loop(0, DEPTH, arrive, jnp.zeros((4, WIDE), F32))
+    out_ref[0:4, :] = total * (1.0 / 16.0)
 
     for copy in packs:
         copy.wait_send()
-    for c in range(CHUNKS):
-        wait_bytes(codes_rx.at[c, pl.ds(0, PLANE - 1)], code_send.at[c])
+    wait_bytes(codes_rx.at[pl.ds(0, PLANE - 1)], code_send)
     wait_bytes(stat_rx.at[pl.ds(0, PLANE - 1)], stat_send)
 
     def sent(j, carry):
-        @pl.when(jnp.logical_or(me != block, j != place))
+        @pl.when(jnp.logical_or(sums != block, j != place))
         def _():
-            wait_bytes(window_rx.at[j], final_send.at[j])
+            wait_bytes(window_tx.at[j], final_send.at[j])
         return carry
 
     lax.fori_loop(0, DEPTH, sent, 0)
+
+
+def unpack(packed_ref, grad_ref, hess_ref, grad_hist_ref, hess_hist_ref):
+    grad_ref[...] = packed_ref[4:6, 0:128]
+    hess_ref[...] = packed_ref[6:8, 0:128]
+    grad_hist_ref[...] = packed_ref[0:2, 0:OWNED]
+    hess_hist_ref[...] = packed_ref[2:4, 0:OWNED]
 
 
 def shards(scores, grades, lengths, bin_codes, node_ids):
     vmem = pl.BlockSpec(memory_space=pltpu.VMEM)
     dma = pltpu.SemaphoreType.DMA
     rows = 2, 128
-    grad, hess, grad_hist, hess_hist = pl.pallas_call(
+    packed = pl.pallas_call(
         kernel,
-        out_shape=[
-            jax.ShapeDtypeStruct(rows, F32),
-            jax.ShapeDtypeStruct(rows, F32),
-            jax.ShapeDtypeStruct((2, OWNED), F32),
-            jax.ShapeDtypeStruct((2, OWNED), F32),
-        ],
-        in_specs=[vmem, vmem, vmem, pl.BlockSpec(memory_space=pl.ANY), vmem],
-        out_specs=[vmem] * 4,
+        out_shape=jax.ShapeDtypeStruct((8, WIDE), F32),
+        in_specs=[pl.BlockSpec(memory_space=pl.ANY)] * 5,
+        out_specs=vmem,
         scratch_shapes=[
+            pltpu.VMEM(rows, F32),
+            pltpu.VMEM(rows, I32),
+            pltpu.VMEM((1, 128), I32),
             pltpu.VMEM((FEATURES, 256), I32),
+            pltpu.VMEM(rows, I32),
             pltpu.VMEM((FEATURES + 4, 2, 128), I32),
-            pltpu.VMEM((CHUNKS, PLANE, PER, 2, 128), I32),
+            pltpu.VMEM((PLANE, SLOTS, 2, 128), I32),
             pltpu.VMEM((2, 2, 128), F32),
             pltpu.VMEM((SPLIT, 2, 2, 128), F32),
             pltpu.VMEM((8, 128), F32),
@@ -369,22 +406,29 @@
             pltpu.VMEM((128 * TILES, 256), F32),
             pltpu.VMEM((128 * TILES, 256), BF16),
             pltpu.VMEM((SLOTS, 4, BINS), F32),
-            pltpu.VMEM((DEPTH, WINDOW, 4, BINS), F32),
-            dma,
+            pltpu.VMEM((DEPTH, 4, WIDE), F32),
+            pltpu.VMEM((DEPTH, 4, WIDE), F32),
+            dma((5,)),
             dma((SPLIT,)),
             dma((SPLIT,)),
-            dma((CHUNKS,)),
-            dma((CHUNKS,)),
+            dma,
+            dma,
             dma,
             dma,
             dma((DEPTH,)),
             dma((DEPTH,)),
         ],
         compiler_params=pltpu.CompilerParams(
-            collective_id=0, has_side_effects=True, vmem_limit_bytes=40 * 2**20
+            collective_id=0, has_side_effects=True, vmem_limit_bytes=60 * 2**20
         ),
         cost_estimate=pl.CostEstimate(flops=10**9, bytes_accessed=10**6, transcendentals=10**6),
     )(scores.reshape(rows), grades.reshape(rows), lengths, bin_codes, node_ids.reshape(rows))
+    grad, hess, grad_hist, hess_hist = pl.pallas_call(
+        unpack,
+        out_shape=[jax.ShapeDtypeStruct(shape, F32) for shape in (rows, rows, (2, OWNED), (2, OWNED))],
+        in_specs=[vmem],
+        out_specs=[vmem] * 4,
+    )(packed)
     return grad.reshape(-1), hess.reshape(-1), grad_hist, hess_hist
 
 

time: 58.8 us -> 49 us (0.83)
  the two profiles are of different devices: /device:TPU:2 before, /device:TPU:131 now
where the time goes in v2:
time: 49 us; the launch traced here: 48.8 us
  Pallas kernels  48.2 us (98%)
  between operations  0.64 us (1%)
    pallas_call x1, Pallas kernels, shards(): pl.pallas_call(kernel, out_shape=jax.ShapeDtypeStruct((8, WIDE), F32), in...  46.9 us
    pallas_call x1, Pallas kernels, shards(): pl.pallas_call(unpack, out_shape=[jax.ShapeDtypeStruct(shape, F32) for sh...  1.3 us

profile of v2, /device:TPU:131, one launch (start us, length us, event | category | flops | bytes accessed | tf_op | source)
XLA Modules:
  0.0 48.8 jit_solution(7759363873279741982)
XLA Ops:
  0.6 46.9 %shard_map.84.packed_ref = f32[8,384]{1,0:T(8,128)} custom-call(f32[2,128]{1,0:T(2,128)} %bitcast.5, s32[2,128]{1,0:T(2,128)} %bitcast.6, s32[1,128]{1,0:T(1,128)} %length_hbm.1, s32[700,256]{1,0:T(8,128)} %codes_hbm.1, s32[2,128]{1,0:T(2,128)} %bitcast.7), custom_call_target="tpu_custom_call" | custom-call | flops 1000000000 | bytes 1000000 | tf_op jit(solution)/shard_map/pallas_call | solution.py:383
  47.5 1.3 %shard_map.85 = (f32[2,128]{1,0:T(2,128)}, f32[2,128]{1,0:T(2,128)}, f32[2,350]{1,0:T(2,128)}, f32[2,350]{1,0:T(2,128)}) custom-call(f32[8,384]{1,0:T(8,128)} %shard_map.84.packed_ref), custom_call_target="tpu_custom_call" | custom-call | tf_op jit(solution)/shard_map/pallas_call | solution.py:426

commit v3 on v2

v3 whole, which is shorter than its diff:
```python
import jax
import jax.numpy as jnp
from jax import lax
from jax.experimental import pallas as pl
from jax.experimental.pallas import tpu as pltpu
from jax.sharding import PartitionSpec as P

F32, I32, BF16 = jnp.float32, jnp.int32, jnp.bfloat16
MESH = pl.DeviceIdType.MESH

FEATURES = 700
BINS = 256
PLANE = 32
ROW = 8
DEPTH = 16
SPLIT = 4
TILES = 8
SLOTS = 24
EARLY = 21
QUAD = 4
LOW = BINS // QUAD
WINDOW = 4
WIDE = 384
OWNED = FEATURES * BINS // (PLANE * DEPTH)
LOG2E = 1.4426950408889634


def pieces(x):
    high = x.astype(BF16)
    rest = x - high.astype(F32)
    middle = rest.astype(BF16)
    return high, middle, (rest - middle.astype(F32)).astype(BF16)


def over_rows(x):
    return jnp.sum(x.reshape(x.shape[0] // 8, 8, x.shape[1]), axis=0)


def inverse(x):
    guess = pl.reciprocal(x, approx=True)
    return guess * (2.0 - x * guess)


def wait_bytes(ref, sem):
    pltpu.make_async_copy(ref, ref, sem).wait()


def feature_block(inner):
    x, core = inner // 2, inner % 2
    return 4 * (x % 2) + 2 * core + x // 2


def kernel(
    score_hbm, grade_hbm, length_hbm, codes_hbm, node_hbm,
    out_ref,
    score_ref, grade_ref, length_ref, codes_in, node_ref,
    codes_tx, codes_rx, pack_tx, pack_rx, stat_tx, stat_rx, split,
    query, discount, score_all, gain_all, col_fixed, col_sent, same, hist, window_rx,
    load_sem, pack_send, pack_recv, code_send, code_recv, stat_send, stat_recv, final_send, final_recv, ready,
):
    dp, part = lax.axis_index("dp"), lax.axis_index("qsplit")
    y, z_low, inner = dp // 32, (dp // 8) % 4, dp % 8
    level = z_low * 4 + part
    sums = y * 8 + feature_block(inner)
    block, place = dp // 4, (dp % 4) * 4 + part

    def near_peer(i):
        return 0, (inner + 1 + i) % ROW

    def far_peer(i):
        step = 1 + (1 + i // ROW) % 3
        return step, (inner + i) % ROW

    def device(peer):
        step, at = peer
        return (((y + step) % 4) * 32 + z_low * 8 + at, part)

    def slot(step):
        return ((4 - step) % 4) * ROW + inner

    loads = []
    for i, (source, target) in enumerate((
        (score_hbm, score_ref), (grade_hbm, grade_ref), (length_hbm, length_ref), (node_hbm, node_ref),
        (codes_hbm, codes_in),
    )):
        loads.append(pltpu.make_async_copy(source, target, load_sem.at[i]))
        loads[-1].start()

    barrier = pltpu.get_barrier_semaphore()

    def greet(peer):
        def body(i, carry):
            pl.semaphore_signal(barrier, inc=1, device_id=device(peer(i)), device_id_type=MESH)
            return carry
        return body

    for r in range(1, SPLIT):
        pl.semaphore_signal(barrier, inc=1, device_id=(dp, (part + r) % SPLIT), device_id_type=MESH)
    def neighbour(r):
        return (y * 32 + ((z_low + r) % 4) * 8 + inner, part)

    for r in range(1, 4):
        pl.semaphore_signal(barrier, inc=1, device_id=neighbour(r), device_id_type=MESH)
    lax.fori_loop(0, PLANE - ROW, greet(far_peer), 0)
    lax.fori_loop(0, ROW - 1, greet(near_peer), 0)

    for load in loads[:4]:
        load.wait()

    gain = ((1 << grade_ref[...]) - 1).astype(F32)
    scaled = score_ref[...] * LOG2E
    pack_tx[0] = scaled
    pack_tx[1] = gain
    pack_rx[0] = pack_tx[...]

    pl.semaphore_wait(barrier, PLANE - 1 + SPLIT - 1 + 3)

    packs = {}
    for r in range(1, SPLIT):
        packs[SPLIT - r] = pltpu.make_async_remote_copy(
            src_ref=pack_tx, dst_ref=pack_rx.at[SPLIT - r],
            send_sem=pack_send.at[SPLIT - r], recv_sem=pack_recv.at[SPLIT - r],
            device_id=(dp, (part + r) % SPLIT), device_id_type=MESH,
        )
    for r in (2, 1, 3):
        packs[r].start()

    loads[4].wait()

    def lay(i, carry):
        at = pl.multiple_of(i * 8, 8)
        for h in range(2):
            codes_tx[pl.ds(at, 8), h, :] = codes_in[pl.ds(at, 8), 128 * h:128 * h + 128]
        return carry

    whole = FEATURES // 8
    lax.fori_loop(0, whole, lay, 0, unroll=4)
    for h in range(2):
        codes_tx[8 * whole:FEATURES, h, :] = codes_in[8 * whole:FEATURES, 128 * h:128 * h + 128]
    codes_tx[FEATURES:FEATURES + 4] = jnp.zeros((4, 2, 128), I32)

    spans = pl.ds(0, EARLY), pl.ds(EARLY, SLOTS - EARLY)

    def codes_for(peer, late):
        step, at = peer
        first = (((y + step) % 4) * 8 + feature_block(at)) * 175 // 8
        return codes_tx.at[pl.ds(first + EARLY, SLOTS - EARLY) if late else pl.ds(first, EARLY)]

    def send_codes(late):
        def body(peer):
            def send(i, carry):
                to = peer(i)
                pltpu.make_async_remote_copy(
                    src_ref=codes_for(to, late), dst_ref=codes_rx.at[slot(to[0]), spans[late]],
                    send_sem=code_send.at[late], recv_sem=code_recv.at[late],
                    device_id=device(to), device_id_type=MESH,
                ).start()
                return carry
            return send

        lax.fori_loop(0, PLANE - ROW, body(far_peer), 0)
        lax.fori_loop(0, ROW - 1, body(near_peer), 0)
        codes_rx[inner, spans[late]] = codes_for((0, inner), late)[...]

    def wait_codes(late, sem):
        wait_bytes(codes_rx.at[pl.ds(0, PLANE - 1), spans[late]], sem.at[late])

    send_codes(0)

    sub = lax.broadcasted_iota(I32, (128, 128), 0)
    lane = lax.broadcasted_iota(I32, (128, 128), 1)
    lengths = jnp.broadcast_to(length_ref[...].astype(F32) * 0.125, (128, 128))
    ends = 8.0 * jnp.dot(
        jnp.where(lane <= sub, lengths, 0.0).astype(BF16), jnp.ones((128, 128), BF16), preferred_element_type=F32
    )
    lane_row = lax.broadcasted_iota(I32, (1, 128), 1).astype(F32)
    for b in range(TILES):
        rows = lane_row + 128.0 * ((2 * part + b) % TILES).astype(F32)
        done = ends <= rows
        query[b:b + 1, :] = jnp.sum(jnp.where(done, 1.0, 0.0), axis=0, keepdims=True)
        first = jnp.max(jnp.where(done, ends, 0.0), axis=0, keepdims=True)
        discount[b:b + 1, :] = 1.0 / jnp.log2(rows - first + 2.0)

    pick_row = lax.broadcasted_iota(I32, (32, 256), 0)
    pick_lane = lax.broadcasted_iota(I32, (32, 256), 1)
    side = (pick_row < 24) == (pick_lane < 128)

    def spread(first, second, out, tiles):
        stack = jnp.concatenate([*pieces(first), second.astype(BF16)], axis=0)
        for b in tiles:
            pick = jnp.where(jnp.logical_and(side, pick_row % 8 == b), 1.0, 0.0).astype(BF16)
            out[128 * b:128 * b + 128, :] = lax.dot_general(
                stack, pick, (((0,), (0,)), ((), ())), preferred_element_type=F32
            )

    spread(discount[...], query[...], col_fixed, range(TILES))
    for b in range(TILES):
        for h in range(2):
            same[128 * b:128 * b + 128, 128 * h:128 * h + 128] = jnp.where(
                col_fixed[128 * b:128 * b + 128, 128:256] == query[h:h + 1, :], 1.0, 0.0
            ).astype(BF16)

    near, far = (0, 1, 2, 3, 6, 7), (4, 5)
    blank = jnp.zeros((2, 128), F32)

    def gather(parts, tiles):
        score_all[...] = jnp.concatenate([pack_rx[r, 0] if r in parts else blank for r in range(SPLIT)], axis=0)
        gain_all[...] = jnp.concatenate([pack_rx[r, 1] if r in parts else blank for r in range(SPLIT)], axis=0)
        spread(score_all[...], gain_all[...], col_sent, tiles)

    def pair(a, b):
        at, row = slice(128 * a, 128 * a + 128), slice(b, b + 1)
        gap = gain_all[row, :] - col_sent[at, 128:256]
        diff = score_all[row, :] - col_sent[at, 0:128]
        power = jnp.exp2(jnp.where(gap < 0.0, -diff, diff))
        ratio = inverse(1.0 + power)
        weight = jnp.where(
            query[row, :] == col_fixed[at, 128:256], jnp.abs(discount[row, :] - col_fixed[at, 0:128]), 0.0
        )
        return gap * (weight * ratio), power * ratio

    nothing = jnp.zeros((8, 128), F32)
    slopes, curves, pushes = [nothing] * 2, [nothing] * 2, [nothing] * TILES

    def own_pairs(tiles):
        for h in range(2):
            for a in tiles:
                slope, other = pair(a, h)
                push = jnp.abs(slope)
                slopes[h] = slopes[h] + over_rows(slope)
                curves[h] = curves[h] + over_rows(push * other)
                pushes[h] = pushes[h] + over_rows(push) * (1.0 if a < 2 else 2.0)

    def other_pairs(a, b):
        slope, _ = pair(a, b)
        pushes[b] = pushes[b] + over_rows(jnp.abs(slope)) * (1.0 if a == b else 2.0)

    packs[1].wait_recv()
    packs[3].wait_recv()
    gather((0, 1, 3), near)
    own_pairs(near)
    for i, b in enumerate((2, 3, 6, 7)):
        for a in (2, 3, 6, 7)[:i + 1]:
            other_pairs(a, b)
    packs[2].wait_recv()

    for r in range(1, 4):
        pl.semaphore_signal(ready, inc=1, device_id=neighbour(r), device_id_type=MESH)
    gather(range(SPLIT), far)
    own_pairs(far)
    for b in far:
        for a in (2, 3, 6, 7, 4, 5)[:b + 1]:
            other_pairs(a, b)
    totals = [jnp.sum(x, axis=0, keepdims=True) for x in pushes]
    stack = jnp.concatenate([*pieces(jnp.concatenate(totals, axis=0)), jnp.zeros((8, 128), BF16)], axis=0)
    stack_row = lax.broadcasted_iota(I32, (32, 128), 0)
    query_total = jnp.zeros((32, 256), F32)
    for b in range(TILES):
        query_total += jnp.dot(
            jnp.where(stack_row % 8 == b, stack, jnp.zeros_like(stack)), same[128 * b:128 * b + 128, :],
            preferred_element_type=F32,
        )
    query_total = jnp.sum(query_total, axis=0, keepdims=True)
    factor = jnp.log2(1.0 + query_total) / jnp.maximum(query_total, 1.0)

    stats = []
    for h in range(2):
        own_factor = factor[:, 128 * h:128 * h + 128]
        grad = -jnp.sum(slopes[h], axis=0, keepdims=True) * own_factor
        hess = jnp.sum(curves[h], axis=0, keepdims=True) * own_factor
        out_ref[4 + h:5 + h, 0:128] = grad
        out_ref[6 + h:7 + h, 0:128] = hess
        node = node_ref[h:h + 1, :]
        for value in (grad, hess):
            for n in range(2):
                stats.append(jnp.where(node == n, value, 0.0))
    stat_tx[...] = jnp.concatenate(stats, axis=0)

    def send_stats(peer):
        def body(i, carry):
            to = peer(i)
            pltpu.make_async_remote_copy(
                src_ref=stat_tx, dst_ref=stat_rx.at[slot(to[0])], send_sem=stat_send, recv_sem=stat_recv,
                device_id=device(to), device_id_type=MESH,
            ).start()
            return carry
        return body

    lax.fori_loop(0, PLANE - ROW, send_stats(far_peer), 0)
    lax.fori_loop(0, ROW - 1, send_stats(near_peer), 0)
    stat_rx[inner] = stat_tx[...]
    send_codes(1)

    def prepare(s, carry):
        value = stat_rx[s]
        high = value.astype(BF16).astype(F32)
        low = value - high
        for h in range(2):
            a, b = high[4 * h:4 * h + 4], low[4 * h:4 * h + 4]
            split[s, :, 128 * h:128 * h + 128] = jnp.concatenate([a, b, a, b], axis=0).astype(BF16)
        return carry

    row16 = lax.broadcasted_iota(I32, (16, 128), 0)
    highs = [(row16 // 8 + 2 * i).astype(BF16) for i in range(QUAD // 2)]
    lows = [(row16 + 16 * i).astype(BF16) for i in range(LOW // 16)]
    one, zero = jnp.ones((16, 128), BF16), jnp.zeros((16, 128), BF16)
    start = (sums * 175 * 32) % BINS

    firsts = [(start + 4 * i * OWNED) // BINS for i in range(4)]

    def slot_at(i):
        first, second, late = firsts[0] + i, firsts[0] + 3, i - 16
        for k in range(4):
            first = jnp.where(i >= 3 * k, firsts[k] + i - 3 * k, first)
            second = jnp.where(i >= 12 + k, firsts[k] + 3, second)
            late = late + jnp.where(late >= firsts[k], 4, 0)
        return jnp.where(i < 12, first, jnp.where(i < 16, second, late))

    plan = [0, 3, 4, 4, 1, 3, 4, 4, 2, 3, 5, 5, 2, 3, 5, 5]

    def operands(slots, s):
        left, right = [], []
        for slot in slots:
            left_half, right_half = [], []
            for h in range(2):
                code = codes_rx[s, slot, h:h + 1, :]
                low = jnp.broadcast_to(code & (LOW - 1), (16, 128)).astype(BF16)
                high = jnp.broadcast_to(code >> 6, (16, 128)).astype(BF16)
                stat = split[s, :, 128 * h:128 * h + 128]
                left_half.append(jnp.concatenate([jnp.where(low == x, one, zero) for x in lows], axis=0))
                right_half.append(jnp.concatenate([jnp.where(high == x, stat, zero) for x in highs], axis=0))
            left.append(jnp.concatenate(left_half, axis=1))
            right.append(jnp.concatenate(right_half, axis=1))
        return jnp.concatenate(left, axis=0), jnp.concatenate(right, axis=0)

    wait_bytes(stat_rx.at[pl.ds(0, PLANE - 1)], stat_recv)
    lax.fori_loop(0, PLANE, prepare, 0, unroll=4)

    wait_codes(0, code_recv)
    pl.semaphore_wait(ready, 3)

    def quad(g, carry):
        slots = [slot_at(g * QUAD + f) for f in range(QUAD)]

        @pl.when(g == SLOTS // QUAD - 1)
        def _():
            wait_codes(1, code_recv)

        both = [operands(slots, s) for s in range(PLANE)]
        table = lax.dot_general(
            jnp.concatenate([a for a, _ in both], axis=1), jnp.concatenate([b for _, b in both], axis=1),
            (((1,), (1,)), ((), ())), preferred_element_type=F32,
        ).T
        for f in range(QUAD):
            for high in range(QUAD):
                r = 8 * (QUAD * f + high)
                halves = table[r:r + 8, LOW * f:LOW * f + LOW]
                hist[2 * slots[f] + high // 2, :, LOW * (high % 2):LOW * (high % 2) + LOW] = halves[0:4] + halves[4:8]

        for j in range(DEPTH):
            @pl.when(g == plan[j])
            def _(j=j):
                window = hist.at[pl.ds((start + j * OWNED) // 128, WINDOW)]
                mine = jnp.logical_and(sums == block, j == place)

                @pl.when(mine)
                def _():
                    window_rx[level] = window[...]

                @pl.when(jnp.logical_not(mine))
                def _():
                    pltpu.make_async_remote_copy(
                        src_ref=window, dst_ref=window_rx.at[level],
                        send_sem=final_send.at[j], recv_sem=final_recv.at[level],
                        device_id=(sums * 4 + j // 4, j % 4), device_id_type=MESH,
                    ).start()
        return carry

    lax.fori_loop(0, SLOTS // QUAD, quad, 0)

    def arrive(k, total):
        @pl.when(jnp.logical_or(sums != block, k != level))
        def _():
            wait_bytes(window_rx.at[k], final_recv.at[k])
        return total + window_rx[k]

    total = lax.fori_loop(0, DEPTH, arrive, jnp.zeros((WINDOW, 4, 128), F32))
    line = jnp.concatenate([total[i] for i in range(WINDOW)], axis=1) * (1.0 / 16.0)
    offset = ((block * 175 * 32) % BINS + place * OWNED) % 128
    out_ref[0:4, :] = pltpu.roll(jnp.concatenate([line, line], axis=0), WINDOW * 128 - offset, 1)[0:4, 0:WIDE]

    for copy in packs.values():
        copy.wait_send()
    wait_codes(0, code_send)
    wait_codes(1, code_send)
    wait_bytes(stat_rx.at[pl.ds(0, PLANE - 1)], stat_send)

    def sent(j, carry):
        @pl.when(jnp.logical_or(sums != block, j != place))
        def _():
            wait_bytes(window_rx.at[j], final_send.at[j])
        return carry

    lax.fori_loop(0, DEPTH, sent, 0)


def unpack(packed_ref, grad_ref, hess_ref, grad_hist_ref, hess_hist_ref):
    grad_ref[...] = packed_ref[4:6, 0:128]
    hess_ref[...] = packed_ref[6:8, 0:128]
    grad_hist_ref[...] = packed_ref[0:2, 0:OWNED]
    hess_hist_ref[...] = packed_ref[2:4, 0:OWNED]


def shards(scores, grades, lengths, bin_codes, node_ids):
    vmem = pl.BlockSpec(memory_space=pltpu.VMEM)
    dma = pltpu.SemaphoreType.DMA
    rows = 2, 128
    packed = pl.pallas_call(
        kernel,
        out_shape=jax.ShapeDtypeStruct((8, WIDE), F32),
        in_specs=[pl.BlockSpec(memory_space=pl.ANY)] * 5,
        out_specs=vmem,
        scratch_shapes=[
            pltpu.VMEM(rows, F32),
            pltpu.VMEM(rows, I32),
            pltpu.VMEM((1, 128), I32),
            pltpu.VMEM((FEATURES, 256), I32),
            pltpu.VMEM(rows, I32),
            pltpu.VMEM((FEATURES + 4, 2, 128), I32),
            pltpu.VMEM((PLANE, SLOTS, 2, 128), I32),
            pltpu.VMEM((2, 2, 128), F32),
            pltpu.VMEM((SPLIT, 2, 2, 128), F32),
            pltpu.VMEM((8, 128), F32),
            pltpu.VMEM((PLANE, 8, 128), F32),
            pltpu.VMEM((PLANE, 16, 256), BF16),
            pltpu.VMEM((8, 128), F32),
            pltpu.VMEM((8, 128), F32),
            pltpu.VMEM((8, 128), F32),
            pltpu.VMEM((8, 128), F32),
            pltpu.VMEM((128 * TILES, 256), F32),
            pltpu.VMEM((128 * TILES, 256), F32),
            pltpu.VMEM((128 * TILES, 256), BF16),
            pltpu.VMEM((2 * SLOTS, 4, 128), F32),
            pltpu.VMEM((DEPTH, WINDOW, 4, 128), F32),
            dma((5,)),
            dma((SPLIT,)),
            dma((SPLIT,)),
            dma((2,)),
            dma((2,)),
            dma,
            dma,
            dma((DEPTH,)),
            dma((DEPTH,)),
            pltpu.SemaphoreType.REGULAR,
        ],
        compiler_params=pltpu.CompilerParams(
            collective_id=0, has_side_effects=True, vmem_limit_bytes=60 * 2**20
        ),
        cost_estimate=pl.CostEstimate(flops=10**9, bytes_accessed=10**6, transcendentals=10**6),
    )(scores.reshape(rows), grades.reshape(rows), lengths, bin_codes, node_ids.reshape(rows))
    grad, hess, grad_hist, hess_hist = pl.pallas_call(
        unpack,
        out_shape=[jax.ShapeDtypeStruct(shape, F32) for shape in (rows, rows, (2, OWNED), (2, OWNED))],
        in_specs=[vmem],
        out_specs=[vmem] * 4,
    )(packed)
    return grad.reshape(-1), hess.reshape(-1), grad_hist, hess_hist


def solution(mesh):
    rows = P(("dp", "qsplit"))
    bins = P(None, ("dp", "qsplit"))
    return jax.shard_map(
        shards,
        mesh=mesh,
        in_specs=(rows, rows, P("dp", None), bins, rows),
        out_specs=(rows, rows, bins, bins),
        check_vma=False,
    )
```

time: 49 us -> 47.6 us (0.971)
  the two profiles are of different devices: /device:TPU:131 before, /device:TPU:2 now
where the time goes in v3:
time: 47.6 us; the launch traced here: 47.4 us
  Pallas kernels  46.7 us (98%)
  between operations  0.64 us (1%)
    pallas_call x1, Pallas kernels, shards(): pl.pallas_call(kernel, out_shape=jax.ShapeDtypeStruct((8, WIDE), F32), in...  45.4 us
    pallas_call x1, Pallas kernels, shards(): pl.pallas_call(unpack, out_shape=[jax.ShapeDtypeStruct(shape, F32) for sh...  1.3 us

profile of v3, /device:TPU:2, one launch (start us, length us, event | category | flops | bytes accessed | tf_op | source)
XLA Modules:
  0.0 47.4 jit_solution(2878150099600470898)
XLA Ops:
  0.6 45.4 %shard_map.84.packed_ref = f32[8,384]{1,0:T(8,128)} custom-call(f32[2,128]{1,0:T(2,128)} %bitcast.5, s32[2,128]{1,0:T(2,128)} %bitcast.6, s32[1,128]{1,0:T(1,128)} %length_hbm.1, s32[700,256]{1,0:T(8,128)} %codes_hbm.1, s32[2,128]{1,0:T(2,128)} %bitcast.7), custom_call_target="tpu_custom_call" | custom-call | flops 1000000000 | bytes 1000000 | tf_op jit(solution)/shard_map/pallas_call | solution.py:418
  46.1 1.3 %shard_map.85 = (f32[2,128]{1,0:T(2,128)}, f32[2,128]{1,0:T(2,128)}, f32[2,350]{1,0:T(2,128)}, f32[2,350]{1,0:T(2,128)}) custom-call(f32[8,384]{1,0:T(8,128)} %shard_map.84.packed_ref), custom_call_target="tpu_custom_call" | custom-call | tf_op jit(solution)/shard_map/pallas_call | solution.py:461

commit v4 on v3

--- a/solution.py
+++ b/solution.py
@@ -16,8 +16,10 @@
 SPLIT = 4
 TILES = 8
 SLOTS = 24
+ORDER = (1, 3, 2, 0)
 EARLY = 21
 QUAD = 4
+AHEAD = 4
 LOW = BINS // QUAD
 WINDOW = 4
 WIDE = 384
@@ -55,7 +57,7 @@
     out_ref,
     score_ref, grade_ref, length_ref, codes_in, node_ref,
     codes_tx, codes_rx, pack_tx, pack_rx, stat_tx, stat_rx, split,
-    query, discount, score_all, gain_all, col_fixed, col_sent, same, hist, window_rx,
+    query, discount, score_all, gain_all, col_fixed, col_sent, same, tables, hist, window_rx,
     load_sem, pack_send, pack_recv, code_send, code_recv, stat_send, stat_recv, final_send, final_recv, ready,
 ):
     dp, part = lax.axis_index("dp"), lax.axis_index("qsplit")
@@ -276,18 +278,18 @@
                 stats.append(jnp.where(node == n, value, 0.0))
     stat_tx[...] = jnp.concatenate(stats, axis=0)
 
-    def send_stats(peer):
+    def send_stats(peer, far):
         def body(i, carry):
             to = peer(i)
             pltpu.make_async_remote_copy(
-                src_ref=stat_tx, dst_ref=stat_rx.at[slot(to[0])], send_sem=stat_send, recv_sem=stat_recv,
+                src_ref=stat_tx, dst_ref=stat_rx.at[slot(to[0])], send_sem=stat_send, recv_sem=stat_recv.at[far],
                 device_id=device(to), device_id_type=MESH,
             ).start()
             return carry
         return body
 
-    lax.fori_loop(0, PLANE - ROW, send_stats(far_peer), 0)
-    lax.fori_loop(0, ROW - 1, send_stats(near_peer), 0)
+    lax.fori_loop(0, PLANE - ROW, send_stats(far_peer, 1), 0)
+    lax.fori_loop(0, ROW - 1, send_stats(near_peer, 0), 0)
     stat_rx[inner] = stat_tx[...]
     send_codes(1)
 
@@ -309,14 +311,14 @@
     firsts = [(start + 4 * i * OWNED) // BINS for i in range(4)]
 
     def slot_at(i):
-        first, second, late = firsts[0] + i, firsts[0] + 3, i - 16
+        first, second, late = i, firsts[0] + 3, i - 16
         for k in range(4):
-            first = jnp.where(i >= 3 * k, firsts[k] + i - 3 * k, first)
+            first = jnp.where(i >= 3 * k, firsts[ORDER[k]] + i - 3 * k, first)
             second = jnp.where(i >= 12 + k, firsts[k] + 3, second)
             late = late + jnp.where(late >= firsts[k], 4, 0)
         return jnp.where(i < 12, first, jnp.where(i < 16, second, late))
 
-    plan = [0, 3, 4, 4, 1, 3, 4, 4, 2, 3, 5, 5, 2, 3, 5, 5]
+    plan = [2, 3, 4, 4, 0, 3, 4, 4, 2, 3, 5, 5, 1, 3, 5, 5]
 
     def operands(slots, s):
         left, right = [], []
@@ -333,24 +335,37 @@
             right.append(jnp.concatenate(right_half, axis=1))
         return jnp.concatenate(left, axis=0), jnp.concatenate(right, axis=0)
 
-    wait_bytes(stat_rx.at[pl.ds(0, PLANE - 1)], stat_recv)
-    lax.fori_loop(0, PLANE, prepare, 0, unroll=4)
-
-    wait_codes(0, code_recv)
-    pl.semaphore_wait(ready, 3)
-
-    def quad(g, carry):
-        slots = [slot_at(g * QUAD + f) for f in range(QUAD)]
+    def product(slots, sources):
+        both = [operands(slots, s) for s in sources]
+        return lax.dot_general(
+            jnp.concatenate([a for a, _ in both], axis=1), jnp.concatenate([b for _, b in both], axis=1),
+            (((1,), (1,)), ((), ())), preferred_element_type=F32,
+        )
+
+    def slots_of(g):
+        return [slot_at(g * QUAD + f) for f in range(QUAD)]
+
+    def near_quad(g, carry):
+        tables[g] = product(slots_of(g), range(ROW))
+        return carry
+
+    def far_quad(g, carry):
+        slots = slots_of(g)
+        finish(g, slots, tables[g] + product(slots, range(ROW, PLANE)))
+        return carry
+
+    def whole_quad(g, carry):
+        slots = slots_of(g)
 
         @pl.when(g == SLOTS // QUAD - 1)
         def _():
             wait_codes(1, code_recv)
 
-        both = [operands(slots, s) for s in range(PLANE)]
-        table = lax.dot_general(
-            jnp.concatenate([a for a, _ in both], axis=1), jnp.concatenate([b for _, b in both], axis=1),
-            (((1,), (1,)), ((), ())), preferred_element_type=F32,
-        ).T
+        finish(g, slots, product(slots, range(PLANE)))
+        return carry
+
+    def finish(g, slots, table):
+        table = table.T
         for f in range(QUAD):
             for high in range(QUAD):
                 r = 8 * (QUAD * f + high)
@@ -374,9 +389,16 @@
                         send_sem=final_send.at[j], recv_sem=final_recv.at[level],
                         device_id=(sums * 4 + j // 4, j % 4), device_id_type=MESH,
                     ).start()
-        return carry
-
-    lax.fori_loop(0, SLOTS // QUAD, quad, 0)
+
+    wait_codes(0, code_recv)
+    wait_bytes(stat_rx.at[pl.ds(0, ROW - 1)], stat_recv.at[0])
+    lax.fori_loop(0, ROW, prepare, 0, unroll=4)
+    lax.fori_loop(0, AHEAD, near_quad, 0)
+    wait_bytes(stat_rx.at[pl.ds(0, PLANE - ROW)], stat_recv.at[1])
+    lax.fori_loop(ROW, PLANE, prepare, 0, unroll=4)
+    pl.semaphore_wait(ready, 3)
+    lax.fori_loop(0, AHEAD, far_quad, 0)
+    lax.fori_loop(AHEAD, SLOTS // QUAD, whole_quad, 0)
 
     def arrive(k, total):
         @pl.when(jnp.logical_or(sums != block, k != level))
@@ -440,6 +462,7 @@
             pltpu.VMEM((128 * TILES, 256), F32),
             pltpu.VMEM((128 * TILES, 256), F32),
             pltpu.VMEM((128 * TILES, 256), BF16),
+            pltpu.VMEM((AHEAD, QUAD * LOW, QUAD * QUAD * 8), F32),
             pltpu.VMEM((2 * SLOTS, 4, 128), F32),
             pltpu.VMEM((DEPTH, WINDOW, 4, 128), F32),
             dma((5,)),
@@ -448,7 +471,7 @@
             dma((2,)),
             dma((2,)),
             dma,
-            dma,
+            dma((2,)),
             dma((DEPTH,)),
             dma((DEPTH,)),
             pltpu.SemaphoreType.REGULAR,

time: 47.6 us -> 46.4 us (0.975)
  Pallas kernels: 46.7 us -> 45.6 us
    pallas_call x1, Pallas kernels: 45.4 us -> 44.3 us  [shards(): pl.pallas_call(kernel, out_shape=jax.ShapeDtypeStruct((8, WIDE), F32), in...]
where the time goes in v4:
time: 46.4 us; the launch traced here: 46.3 us
  Pallas kernels  45.6 us (98%)
  between operations  0.64 us (1%)
    pallas_call x1, Pallas kernels, shards(): pl.pallas_call(kernel, out_shape=jax.ShapeDtypeStruct((8, WIDE), F32), in...  44.3 us
    pallas_call x1, Pallas kernels, shards(): pl.pallas_call(unpack, out_shape=[jax.ShapeDtypeStruct(shape, F32) for sh...  1.3 us

profile of v4, /device:TPU:2, one launch (start us, length us, event | category | flops | bytes accessed | tf_op | source)
XLA Modules:
  0.0 46.3 jit_solution(6696593049104869662)
XLA Ops:
  0.6 44.3 %shard_map.84.packed_ref = f32[8,384]{1,0:T(8,128)} custom-call(f32[2,128]{1,0:T(2,128)} %bitcast.5, s32[2,128]{1,0:T(2,128)} %bitcast.6, s32[1,128]{1,0:T(1,128)} %length_hbm.1, s32[700,256]{1,0:T(8,128)} %codes_hbm.1, s32[2,128]{1,0:T(2,128)} %bitcast.7), custom_call_target="tpu_custom_call" | custom-call | flops 1000000000 | bytes 1000000 | tf_op jit(solution)/shard_map/pallas_call | solution.py:440
  45.0 1.3 %shard_map.85 = (f32[2,128]{1,0:T(2,128)}, f32[2,128]{1,0:T(2,128)}, f32[2,350]{1,0:T(2,128)}, f32[2,350]{1,0:T(2,128)}) custom-call(f32[8,384]{1,0:T(8,128)} %shard_map.84.packed_ref), custom_call_target="tpu_custom_call" | custom-call | tf_op jit(solution)/shard_map/pallas_call | solution.py:484

commit v5 on v4

--- a/solution.py
+++ b/solution.py
@@ -80,6 +80,21 @@
     def slot(step):
         return ((4 - step) % 4) * ROW + inner
 
+    barrier = pltpu.get_barrier_semaphore()
+
+    def greet(peer):
+        def body(i, carry):
+            pl.semaphore_signal(barrier, inc=1, device_id=device(peer(i)), device_id_type=MESH)
+            return carry
+        return body
+
+    for r in (2, 1, 3):
+        pl.semaphore_signal(barrier, inc=1, device_id=(dp, (part + r) % SPLIT), device_id_type=MESH)
+    def neighbour(r):
+        return (y * 32 + ((z_low + r) % 4) * 8 + inner, part)
+
+    for r in range(1, 4):
+        pl.semaphore_signal(barrier, inc=1, device_id=neighbour(r), device_id_type=MESH)
     loads = []
     for i, (source, target) in enumerate((
         (score_hbm, score_ref), (grade_hbm, grade_ref), (length_hbm, length_ref), (node_hbm, node_ref),
@@ -88,21 +103,6 @@
         loads.append(pltpu.make_async_copy(source, target, load_sem.at[i]))
         loads[-1].start()
 
-    barrier = pltpu.get_barrier_semaphore()
-
-    def greet(peer):
-        def body(i, carry):
-            pl.semaphore_signal(barrier, inc=1, device_id=device(peer(i)), device_id_type=MESH)
-            return carry
-        return body
-
-    for r in range(1, SPLIT):
-        pl.semaphore_signal(barrier, inc=1, device_id=(dp, (part + r) % SPLIT), device_id_type=MESH)
-    def neighbour(r):
-        return (y * 32 + ((z_low + r) % 4) * 8 + inner, part)
-
-    for r in range(1, 4):
-        pl.semaphore_signal(barrier, inc=1, device_id=neighbour(r), device_id_type=MESH)
     lax.fori_loop(0, PLANE - ROW, greet(far_peer), 0)
     lax.fori_loop(0, ROW - 1, greet(near_peer), 0)
 
@@ -149,23 +149,23 @@
         return codes_tx.at[pl.ds(first + EARLY, SLOTS - EARLY) if late else pl.ds(first, EARLY)]
 
     def send_codes(late):
-        def body(peer):
+        def body(peer, far):
             def send(i, carry):
                 to = peer(i)
                 pltpu.make_async_remote_copy(
                     src_ref=codes_for(to, late), dst_ref=codes_rx.at[slot(to[0]), spans[late]],
-                    send_sem=code_send.at[late], recv_sem=code_recv.at[late],
+                    send_sem=code_send.at[2 * late + far], recv_sem=code_recv.at[2 * late + far],
                     device_id=device(to), device_id_type=MESH,
                 ).start()
                 return carry
             return send
 
-        lax.fori_loop(0, PLANE - ROW, body(far_peer), 0)
-        lax.fori_loop(0, ROW - 1, body(near_peer), 0)
+        lax.fori_loop(0, ROW - 1, body(near_peer, 0), 0)
+        lax.fori_loop(0, PLANE - ROW, body(far_peer, 1), 0)
         codes_rx[inner, spans[late]] = codes_for((0, inner), late)[...]
 
-    def wait_codes(late, sem):
-        wait_bytes(codes_rx.at[pl.ds(0, PLANE - 1), spans[late]], sem.at[late])
+    def wait_codes(late, far, sem):
+        wait_bytes(codes_rx.at[pl.ds(0, PLANE - ROW if far else ROW - 1), spans[late]], sem.at[2 * late + far])
 
     send_codes(0)
 
@@ -359,7 +359,8 @@
 
         @pl.when(g == SLOTS // QUAD - 1)
         def _():
-            wait_codes(1, code_recv)
+            wait_codes(1, 0, code_recv)
+            wait_codes(1, 1, code_recv)
 
         finish(g, slots, product(slots, range(PLANE)))
         return carry
@@ -390,12 +391,13 @@
                         device_id=(sums * 4 + j // 4, j % 4), device_id_type=MESH,
                     ).start()
 
-    wait_codes(0, code_recv)
+    wait_codes(0, 0, code_recv)
     wait_bytes(stat_rx.at[pl.ds(0, ROW - 1)], stat_recv.at[0])
     lax.fori_loop(0, ROW, prepare, 0, unroll=4)
     lax.fori_loop(0, AHEAD, near_quad, 0)
     wait_bytes(stat_rx.at[pl.ds(0, PLANE - ROW)], stat_recv.at[1])
     lax.fori_loop(ROW, PLANE, prepare, 0, unroll=4)
+    wait_codes(0, 1, code_recv)
     pl.semaphore_wait(ready, 3)
     lax.fori_loop(0, AHEAD, far_quad, 0)
     lax.fori_loop(AHEAD, SLOTS // QUAD, whole_quad, 0)
@@ -413,8 +415,9 @@
 
     for copy in packs.values():
         copy.wait_send()
-    wait_codes(0, code_send)
-    wait_codes(1, code_send)
+    for late in range(2):
+        for far in range(2):
+            wait_codes(late, far, code_send)
     wait_bytes(stat_rx.at[pl.ds(0, PLANE - 1)], stat_send)
 
     def sent(j, carry):
@@ -468,8 +471,8 @@
             dma((5,)),
             dma((SPLIT,)),
             dma((SPLIT,)),
-            dma((2,)),
-            dma((2,)),
+            dma((4,)),
+            dma((4,)),
             dma,
             dma((2,)),
             dma((DEPTH,)),

time: 46.4 us -> 46.4 us (level)
  no operation moved by 1% of the time
where the time goes in v5:
time: 46.4 us; the launch traced here: 46.2 us
  Pallas kernels  45.6 us (98%)
  between operations  0.64 us (1%)
    pallas_call x1, Pallas kernels, shards(): pl.pallas_call(kernel, out_shape=jax.ShapeDtypeStruct((8, WIDE), F32), in...  44.3 us
    pallas_call x1, Pallas kernels, shards(): pl.pallas_call(unpack, out_shape=[jax.ShapeDtypeStruct(shape, F32) for sh...  1.3 us

profile of v5, /device:TPU:2, one launch (start us, length us, event | category | flops | bytes accessed | tf_op | source)
XLA Modules:
  0.0 46.2 jit_solution(12285751999404451410)
XLA Ops:
  0.6 44.3 %shard_map.84.packed_ref = f32[8,384]{1,0:T(8,128)} custom-call(f32[2,128]{1,0:T(2,128)} %bitcast.5, s32[2,128]{1,0:T(2,128)} %bitcast.6, s32[1,128]{1,0:T(1,128)} %length_hbm.1, s32[700,256]{1,0:T(8,128)} %codes_hbm.1, s32[2,128]{1,0:T(2,128)} %bitcast.7), custom_call_target="tpu_custom_call" | custom-call | flops 1000000000 | bytes 1000000 | tf_op jit(solution)/shard_map/pallas_call | solution.py:443
  44.9 1.3 %shard_map.85 = (f32[2,128]{1,0:T(2,128)}, f32[2,128]{1,0:T(2,128)}, f32[2,350]{1,0:T(2,128)}, f32[2,350]{1,0:T(2,128)}) custom-call(f32[8,384]{1,0:T(8,128)} %shard_map.84.packed_ref), custom_call_target="tpu_custom_call" | custom-call | tf_op jit(solution)/shard_map/pallas_call | solution.py:487
